TPU v7x, 32 devices: a whole 2x2x4 slice. The times are simulated.
32 devices in a mesh: occ: 8 (over y, x, core), virt: 4 (over z).
Axes of the slice: x: 2, y: 2, z: 4, core: 2. Of those that a mesh axis runs over, the one named last changes fastest.
Arguments:
- amplitudes: bfloat16 [4096, 1024], P('occ'), may hold values from -6 to 6
- amp_map: int32 [64, 8], P('occ'), may hold values 0 or 1
- integrals: bfloat16 [1024, 1024], P('occ', 'virt'), may hold values from -0.1875 to 0.1875
- int_map: int32 [8, 8], P(None, 'virt'), may hold values 0 or 1
- exchange: bfloat16 [4096, 1024], P('occ', 'virt'), may hold values from -0.1875 to 0.1875
- residual_in: float32 [4096, 1024], P('occ', 'virt'), may hold values from -6 to 6
Outputs:
- residual: float32 [4096, 1024], P('occ', 'virt')
- pair_energy: float32 [4096], P('occ')
All inputs are finite; a program needn't handle non-finite values. No bound on the sum of `amp_map` or of `int_map` on one device may be relied on, other than what follows from the above.
Results may differ from a plain program's by a relative error of at most 0.0003.
Values may be sent and summed in bfloat16 or wider, within the bound.
A program may use at most 64 MiB of HBM per device.

v0:
```python
import jax
import jax.numpy as jnp
from jax import lax
from jax.sharding import PartitionSpec as P

PTILE = 64
VTILE = 128


def on_device(amplitudes, amp_map, integrals, int_map, exchange, residual_in):
    row_tiles = amp_map.shape[0]
    col_tiles = amp_map.shape[1]
    shaped = amplitudes.reshape(row_tiles, PTILE, col_tiles, VTILE)
    amp_masked = (shaped * amp_map.astype(jnp.bfloat16)[:, None, :, None]).reshape(amplitudes.shape)
    full_mask = jnp.repeat(jnp.repeat(int_map, VTILE, axis=0), VTILE, axis=1).astype(jnp.bfloat16)
    panel = lax.all_gather(integrals, "occ", axis=0, tiled=True)
    product = jnp.dot(amp_masked, panel * full_mask, preferred_element_type=jnp.float32)
    residual = residual_in + product
    energy_terms = jnp.sum(residual * exchange.astype(jnp.float32), axis=1)
    pair_energy = lax.psum(energy_terms, "virt")
    return (residual, pair_energy)


def solution(mesh):
    in_specs = (
        P("occ", None),
        P("occ", None),
        P("occ", "virt"),
        P(None, "virt"),
        P("occ", "virt"),
        P("occ", "virt"),
    )
    out_specs = (P("occ", "virt"), P("occ"))
    return jax.shard_map(
        on_device, mesh=mesh, in_specs=in_specs, out_specs=out_specs, check_vma=False
    )
```

profile of v0, /device:TPU:0, one launch (start us, length us, event | category | flops | bytes accessed | tf_op | source)
XLA Modules:
  0.0 31.2 jit_solution(522073076555580517)
XLA Ops:
  0.6 0.0 copy-start.4
  0.6 0.7 %convert_element_type.18 = bf16[8,2]{0,1:T(2,128)(2,1)S(1)} convert(s32[8,2]{0,1:T(2,128)} %param.9) | non-fusion elementwise | flops 16 | bytes 96 | tf_op jit(solution)/shard_map/convert_element_type | solution.py:15
  1.3 0.1 copy.8
  1.4 0.0 copy-done.4
  1.5 0.0 copy-start.2
  1.5 0.0 copy-start.3
  1.5 2.9 %broadcast_in_dim.8 = bf16[1024,2,128]{2,1,0:T(2,128)(2,1)S(1)} broadcast(bf16[1024,2]{1,0:T(8,128)(2,1)S(1)} %bitcast.16), dimensions={0,1} | broadcast | bytes 528384 | tf_op jit(solution)/shard_map/broadcast_in_dim | solution.py:15
  4.4 0.0 copy-done.2
  4.5 0.0 copy-start.1
  4.5 0.1 copy.10
  4.6 0.0 copy-done.3
  4.6 11.3 %all_gather.3 = bf16[1024,256]{1,0:T(8,128)(2,1)S(1)} all-gather(bf16[128,256]{1,0:T(8,128)(2,1)S(1)} %copy-done.3), channel_id=1, replica_groups=mesh['occ'=8,'virt'=4] {'occ'}, dimensions={0}, use_global_device_ids=true | all-gather | bytes 589824 | tf_op jit(solution)/shard_map/all_gather | solution.py:16
  15.9 0.0 copy-done.1
  15.9 0.0 copy-start
  15.9 0.2 copy.9
  16.2 0.2 mul.17
  16.4 0.8 %copy-done = bf16[512,1024]{1,0:T(8,128)(2,1)S(1)} copy-done((bf16[512,1024]{1,0:T(8,128)(2,1)S(1)}, bf16[512,1024]{1,0:T(8,128)(2,1)}, u32[]{:S(2)}) %copy-start) | copy-done | bytes 1048600
  17.2 0.5 %multiply_reduce_fusion = (f32[512]{0:T(512)S(1)}, f32[512,256]{0,1:T(8,128)S(1)}) fusion(bf16[512,256]{0,1:T(8,128)(2,1)S(1)} %copy.10, f32[512,256]{0,1:T(8,128)S(1)} %copy.9, bf16[1024,256]{1,0:T(8,128)(2,1)S(1)} %all_gather.3, bf16[128,8,2,128]{3,2,1,0:T(2,128)(2,1)S(1)} %bitcast.15, bf16[512,1024]{1,0:T(8,128)(2,1)S(1)} %copy-done, ...), kind=kOutput, calls=%fused_computation.5 | convolution fusion | flops 269745664 | bytes 4458496 | tf_op jit(solution)/shard_map/dot_general | solution.py:17
  17.7 12.5 %psum.7 = f32[512]{0:T(512)} all-reduce(f32[512]{0:T(512)S(1)} %get-tuple-element.4), channel_id=1, replica_groups=mesh['occ'=8,'virt'=4] {'virt'}, use_global_device_ids=true, to_apply=%region_1.0 | all-reduce | flops 512 | bytes 4096 | tf_op jit(solution)/shard_map/psum | solution.py:20
  30.2 1.0 %copy.11 = f32[512,256]{1,0:T(8,128)} copy(f32[512,256]{0,1:T(8,128)S(1)} %get-tuple-element.5) | data formatting | bytes 1048576
  (2 shorter events, 0.0 us)
Async XLA Ops:
  0.6 0.8 %copy-start.4 = (s32[8,8]{1,0:T(8,128)S(1)}, s32[8,8]{1,0:T(8,128)}, u32[]{:S(2)}) copy-start(s32[8,8]{1,0:T(8,128)} %param.7) | copy-start | bytes 772
  1.5 3.0 %copy-start.2 = (bf16[512,256]{1,0:T(8,128)(2,1)S(1)}, bf16[512,256]{1,0:T(8,128)(2,1)}, u32[]{:S(2)}) copy-start(bf16[512,256]{1,0:T(8,128)(2,1)} %param.10) | copy-start | bytes 786436
  1.5 3.1 %copy-start.3 = (bf16[128,256]{1,0:T(8,128)(2,1)S(1)}, bf16[128,256]{1,0:T(8,128)(2,1)}, u32[]{:S(2)}) copy-start(bf16[128,256]{1,0:T(8,128)(2,1)} %param.8) | copy-start | bytes 196612
  4.5 11.5 %copy-start.1 = (f32[512,256]{1,0:T(8,128)S(1)}, f32[512,256]{1,0:T(8,128)}, u32[]{:S(2)}) copy-start(f32[512,256]{1,0:T(8,128)} %param.11) | copy-start | bytes 1572868
  15.9 1.2 %copy-start = (bf16[512,1024]{1,0:T(8,128)(2,1)S(1)}, bf16[512,1024]{1,0:T(8,128)(2,1)}, u32[]{:S(2)}) copy-start(bf16[512,1024]{1,0:T(8,128)(2,1)} %param.6) | copy-start | bytes 3145732
where the time goes:
time: 31.5 us; the launch traced here: 31.2 us
  blocking collectives  23.8 us (76%)
  local copies, waits for them, and re-layouts  5.44 us (17%)
  between operations  0.72 us (2%)
  other arithmetic  0.69 us (2%)
  matrix products  0.53 us (2%)
    psum x1, blocking collectives, on_device(): pair_energy = lax.psum(energy_terms, 'virt')  12.5 us
    all_gather x1, blocking collectives, on_device(): panel = lax.all_gather(integrals, 'occ', axis=0, tiled=True)  11.3 us
    broadcast_in_dim x1, local copies, waits for them, and re-layouts, on_device(): jnp.repeat(jnp.repeat(int_map, VTILE, axis=0), VTILE, axis=1)  2.94 us
    unnamed x13, local copies, waits for them, and re-layouts  2.16 us
    convert_element_type x1, other arithmetic, on_device(): jnp.repeat(jnp.repeat(int_map, VTILE, axis=0), VTILE, axis=1)  0.69 us

commit v1 on v0

v1 whole, which is shorter than its diff:
```python
import functools

import jax
import jax.numpy as jnp
from jax import lax
from jax.experimental import pallas as pl
from jax.experimental.pallas import tpu as pltpu
from jax.sharding import PartitionSpec as P

PTILE = 64
VTILE = 128
LANES = 128
MESH = pl.DeviceIdType.MESH


def flipped(index, bits):
    out, place = 0, 1
    top = 0
    while place <= bits:
        digit = lax.rem(index // place, 2)
        flip = (bits // place) % 2
        out = out + (1 - digit if flip else digit) * place
        place *= 2
        top = place
    return out + (index // top) * top if top else index


def kernel(
    n, nv,
    amp_hbm, amap_hbm, int_hbm, imap_hbm, exch_hbm, res_hbm,
    out_ref, energy_ref,
    amp, amap, panel, imap, exch, acc, slots,
    in_sem, core_send, core_recv, chip_send, chip_recv, en_send, en_recv,
):
    me = lax.axis_index("occ")
    mv = lax.axis_index("virt")
    chips = n // 2
    chip, core = me // 2, lax.rem(me, 2)
    mate = chip * 2 + (1 - core)
    depth = int_hbm.shape[0]
    rows, cols = out_ref.shape

    def block(owner):
        return panel.at[pl.ds(pl.multiple_of(owner * depth, depth), depth), :]

    loads = [
        pltpu.make_async_copy(int_hbm, block(me), in_sem.at[0]),
        pltpu.make_async_copy(imap_hbm, imap, in_sem.at[1]),
        pltpu.make_async_copy(amp_hbm, amp, in_sem.at[2]),
        pltpu.make_async_copy(amap_hbm, amap, in_sem.at[3]),
        pltpu.make_async_copy(res_hbm, acc, in_sem.at[4]),
        pltpu.make_async_copy(exch_hbm, exch, in_sem.at[5]),
    ]
    for load in loads:
        load.start()

    partners = [flipped(chip, s) for s in range(chips)]
    barrier = pltpu.get_barrier_semaphore()
    pl.semaphore_signal(barrier, inc=1, device_id=(mate, mv), device_id_type=MESH)
    for s in range(1, chips):
        pl.semaphore_signal(barrier, inc=1, device_id=(partners[s] * 2 + core, mv), device_id_type=MESH)
    for s in range(1, nv):
        pl.semaphore_signal(barrier, inc=1, device_id=(me, lax.rem(mv + s, nv)), device_id_type=MESH)

    loads[0].wait()
    loads[1].wait()
    grain = min(depth, VTILE)
    while depth % grain or VTILE % grain:
        grain //= 2
    for t in range(depth // grain):
        tile = (me * depth + t * grain) // VTILE
        here = pl.ds(pl.multiple_of(me * depth + t * grain, grain), grain)
        for c in range(cols // VTILE):
            wide = pl.ds(c * VTILE, VTILE)
            keep = imap[c, tile].astype(jnp.float32).astype(jnp.bfloat16)
            panel[here, wide] = panel[here, wide] * keep

    pl.semaphore_wait(barrier, chips + nv - 1)

    def to_mate(s):
        owner = partners[s] * 2 + core
        return pltpu.make_async_remote_copy(
            src_ref=block(owner), dst_ref=block(owner),
            send_sem=core_send.at[s], recv_sem=core_recv.at[s],
            device_id=(mate, mv), device_id_type=MESH,
        )

    def to_chip(s):
        return pltpu.make_async_remote_copy(
            src_ref=block(me), dst_ref=block(me),
            send_sem=chip_send.at[s], recv_sem=chip_recv.at[s],
            device_id=(partners[s] * 2 + core, mv), device_id_type=MESH,
        )

    def from_chip(s):
        owner = partners[s] * 2 + core
        return pltpu.make_async_remote_copy(
            src_ref=block(owner), dst_ref=block(owner),
            send_sem=chip_send.at[s], recv_sem=chip_recv.at[s],
            device_id=(partners[s] * 2 + core, mv), device_id_type=MESH,
        )

    def from_mate(s):
        owner = partners[s] * 2 + (1 - core)
        return pltpu.make_async_remote_copy(
            src_ref=block(owner), dst_ref=block(owner),
            send_sem=core_send.at[s], recv_sem=core_recv.at[s],
            device_id=(mate, mv), device_id_type=MESH,
        )

    chip_copies = [None] + [to_chip(s) for s in range(1, chips)]
    mate_copies = [to_mate(s) for s in range(chips)]
    for s in range(1, chips):
        chip_copies[s].start()
    mate_copies[0].start()

    loads[2].wait()
    loads[3].wait()
    for r in range(rows // PTILE):
        tall = pl.ds(r * PTILE, PTILE)
        for k in range(amp.shape[1] // VTILE):
            wide = pl.ds(k * VTILE, VTILE)
            keep = amap[r, k].astype(jnp.float32).astype(jnp.bfloat16)
            amp[tall, wide] = amp[tall, wide] * keep
    loads[4].wait()
    loads[5].wait()

    def product(s):
        span = 2 * depth
        start = partners[s] * span
        return jnp.dot(
            amp[:, pl.ds(pl.multiple_of(start, LANES), span)],
            panel[pl.ds(pl.multiple_of(start, LANES), span), :],
            preferred_element_type=jnp.float32,
        )

    for s in range(chips):
        if s + 1 < chips:
            if s == 0:
                from_mate(0).wait_recv()
                acc[...] += product(0)
            from_chip(s + 1).wait_recv()
            mate_copies[s + 1].start()
        if s > 0:
            from_mate(s).wait_recv()
            if s < chips - 1:
                acc[...] += product(s)

    residual = acc[...] + product(chips - 1)
    out_ref[...] = residual
    terms = residual * exch[...].astype(jnp.float32)
    folded = terms[:, :LANES]
    for c in range(1, cols // LANES):
        folded = folded + terms[:, c * LANES:(c + 1) * LANES]
    for q in range(rows // LANES):
        part = folded[q * LANES:(q + 1) * LANES, :].T
        slots[mv, pl.ds(q, 1), :] = jnp.sum(part, axis=0, keepdims=True)

    sends = []
    for s in range(1, nv):
        send = pltpu.make_async_remote_copy(
            src_ref=slots.at[mv], dst_ref=slots.at[mv],
            send_sem=en_send.at[s], recv_sem=en_recv.at[s],
            device_id=(me, lax.rem(mv + s, nv)), device_id_type=MESH,
        )
        send.start()
        sends.append(send)
    for s in range(1, nv):
        origin = lax.rem(mv + nv - s, nv)
        pltpu.make_async_remote_copy(
            src_ref=slots.at[origin], dst_ref=slots.at[origin],
            send_sem=en_send.at[s], recv_sem=en_recv.at[s],
            device_id=(me, origin), device_id_type=MESH,
        ).wait_recv()
    total = slots[0]
    for v in range(1, nv):
        total = total + slots[v]
    energy_ref[...] = total

    for send in sends:
        send.wait_send()
    for s in range(1, chips):
        chip_copies[s].wait_send()
    for s in range(chips):
        mate_copies[s].wait_send()


def solution(mesh):
    n, nv = mesh.shape["occ"], mesh.shape["virt"]
    chips = n // 2

    def on_device(amplitudes, amp_map, integrals, int_map, exchange, residual_in):
        rows, k = amplitudes.shape
        depth, cols = integrals.shape
        imap = int_map.T
        held = 2 * rows * k + 2 * k * cols + 2 * rows * cols + 8 * rows * cols
        hbm = pl.BlockSpec(memory_space=pltpu.HBM)
        vmem = pl.BlockSpec(memory_space=pltpu.VMEM)
        residual, energy = pl.pallas_call(
            functools.partial(kernel, n, nv),
            out_shape=(
                jax.ShapeDtypeStruct((rows, cols), jnp.float32),
                jax.ShapeDtypeStruct((rows // LANES, LANES), jnp.float32),
            ),
            in_specs=[hbm] * 6,
            out_specs=(vmem, vmem),
            scratch_shapes=[
                pltpu.VMEM((rows, k), jnp.bfloat16),
                pltpu.SMEM(amp_map.shape, jnp.int32),
                pltpu.VMEM((k, cols), jnp.bfloat16),
                pltpu.SMEM(imap.shape, jnp.int32),
                pltpu.VMEM((rows, cols), jnp.bfloat16),
                pltpu.VMEM((rows, cols), jnp.float32),
                pltpu.VMEM((nv, rows // LANES, LANES), jnp.float32),
                pltpu.SemaphoreType.DMA((6,)),
                pltpu.SemaphoreType.DMA((chips,)),
                pltpu.SemaphoreType.DMA((chips,)),
                pltpu.SemaphoreType.DMA((chips,)),
                pltpu.SemaphoreType.DMA((chips,)),
                pltpu.SemaphoreType.DMA((nv,)),
                pltpu.SemaphoreType.DMA((nv,)),
            ],
            compiler_params=pltpu.CompilerParams(
                collective_id=0, has_side_effects=True, vmem_limit_bytes=held + (8 << 20)
            ),
            cost_estimate=pl.CostEstimate(flops=2 * rows * k * cols, bytes_accessed=held, transcendentals=0),
        )(amplitudes, amp_map, integrals, imap, exchange, residual_in)
        return residual, energy.reshape(rows)

    in_specs = (
        P("occ", None),
        P("occ", None),
        P("occ", "virt"),
        P(None, "virt"),
        P("occ", "virt"),
        P("occ", "virt"),
    )
    out_specs = (P("occ", "virt"), P("occ"))
    return jax.shard_map(on_device, mesh=mesh, in_specs=in_specs, out_specs=out_specs, check_vma=False)
```

time: 31.5 us -> 22.9 us (0.73)
  blocking collectives: 23.8 us -> 0 us
  Pallas kernels: 0 us -> 15.2 us
  local copies, waits for them, and re-layouts: 5.44 us -> 6.79 us
  other arithmetic: 0.69 us -> 0 us
  matrix products: 0.53 us -> 0 us
    pallas_call x0 -> x1, Pallas kernels: none -> 15.2 us  [on_device(): pl.pallas_call(functools.partial(kernel, n, nv), out_shape=(jax.ShapeDtyp...]
    psum x1 -> x0, blocking collectives: 12.5 us -> none  [on_device(): pair_energy = lax.psum(energy_terms, 'virt')]
    all_gather x1 -> x0, blocking collectives: 11.3 us -> none  [on_device(): panel = lax.all_gather(integrals, 'occ', axis=0, tiled=True)]
    unnamed x13 -> x14, local copies, waits for them, and re-layouts: 2.16 us -> 6.79 us
    broadcast_in_dim x2 -> x0, local copies, waits for them, and re-layouts: 2.98 us -> none  [the longest x1 2.94 us: on_device(): jnp.repeat(jnp.repeat(int_map, VTILE, axis=0), VTILE, axis=1)]
    convert_element_type x2 -> x0, other arithmetic: 0.69 us -> none  [the longest x1 0.69 us: on_device(): jnp.repeat(jnp.repeat(int_map, VTILE, axis=0), VTILE, axis=1)]
    dot_general x1 -> x0, matrix products: 0.53 us -> none  [on_device(): jnp.dot(amp_masked, panel * full_mask, preferred_element_type=jnp.float32)]
where the time goes in v1:
time: 22.9 us; the launch traced here: 22.6 us
  Pallas kernels  15.2 us (66%)
  local copies, waits for them, and re-layouts  6.79 us (30%)
  between operations  0.65 us (3%)
    pallas_call x1, Pallas kernels, on_device(): pl.pallas_call(functools.partial(kernel, n, nv), out_shape=(jax.ShapeDtyp...  15.2 us
    unnamed x14, local copies, waits for them, and re-layouts  6.79 us

profile of v1, /device:TPU:0, one launch (start us, length us, event | category | flops | bytes accessed | tf_op | source)
XLA Modules:
  0.0 22.6 jit_solution(14159036656095756801)
XLA Ops:
  0.6 0.0 copy-start.5
  0.6 0.7 %copy-done.5 = s32[8,2]{0,1:T(2,128)S(1)} copy-done((s32[8,2]{0,1:T(2,128)S(1)}, s32[8,2]{0,1:T(2,128)}, u32[]{:S(2)}) %copy-start.5) | copy-done | bytes 88
  1.3 0.0 copy-start
  1.3 1.2 %copy-done = bf16[512,1024]{1,0:T(8,128)(2,1)S(1)} copy-done((bf16[512,1024]{1,0:T(8,128)(2,1)S(1)}, bf16[512,1024]{1,0:T(8,128)(2,1)}, u32[]{:S(2)}) %copy-start) | copy-done | bytes 1048600
  2.5 0.0 copy-start.1
  2.5 1.0 %copy-done.1 = f32[512,256]{1,0:T(8,128)S(1)} copy-done((f32[512,256]{1,0:T(8,128)S(1)}, f32[512,256]{1,0:T(8,128)}, u32[]{:S(2)}) %copy-start.1) | copy-done | bytes 524312
  3.6 0.0 copy-start.2
  3.6 0.9 %copy-done.2 = bf16[512,256]{1,0:T(8,128)(2,1)S(1)} copy-done((bf16[512,256]{1,0:T(8,128)(2,1)S(1)}, bf16[512,256]{1,0:T(8,128)(2,1)}, u32[]{:S(2)}) %copy-start.2) | copy-done | bytes 262168
  4.5 0.0 copy-start.3
  4.5 0.8 %copy-done.3 = bf16[128,256]{1,0:T(8,128)(2,1)S(1)} copy-done((bf16[128,256]{1,0:T(8,128)(2,1)S(1)}, bf16[128,256]{1,0:T(8,128)(2,1)}, u32[]{:S(2)}) %copy-start.3) | copy-done | bytes 65560
  5.4 0.0 copy-start.4
  5.4 0.7 %copy-done.4 = s32[8,8]{1,0:T(8,128)S(1)} copy-done((s32[8,8]{1,0:T(8,128)S(1)}, s32[8,8]{1,0:T(8,128)}, u32[]{:S(2)}) %copy-start.4) | copy-done | bytes 280
  6.1 15.2 %shard_map.77 = (f32[512,256]{1,0:T(8,128)S(1)}, f32[4,128]{1,0:T(4,128)S(1)}) custom-call(bf16[512,1024]{1,0:T(8,128)(2,1)S(1)} %copy-done, s32[8,8]{1,0:T(8,128)S(1)} %copy-done.4, bf16[128,256]{1,0:T(8,128)(2,1)S(1)} %copy-done.3, s32[2,8]{1,0:T(2,128)S(1)} %bitcast.3, bf16[512,256]{1,0:T(8,128)(2,1)S(1)} %copy-done.2, f32[512,256]{1,0:T(8,128)S(1)} %copy-done.1), custom_call_target="tpu_custom_call" | custom-call | flops 268435456 | bytes 2883584 | tf_op jit(solution)/shard_map/pallas_call | solution.py:199
  21.2 0.8 %copy.10 = f32[512,256]{1,0:T(8,128)} copy(f32[512,256]{1,0:T(8,128)S(1)} %get-tuple-element.8) | data formatting | bytes 1048576
  22.0 0.6 %copy.11 = f32[512]{0:T(512)} copy(f32[512]{0:T(512)S(1)} %bitcast.2) | data formatting | bytes 4096
Async XLA Ops:
  0.6 0.7 %copy-start.5 = (s32[8,2]{0,1:T(2,128)S(1)}, s32[8,2]{0,1:T(2,128)}, u32[]{:S(2)}) copy-start(s32[8,2]{0,1:T(2,128)} %param.9) | copy-start | bytes 196
  1.3 1.2 %copy-start = (bf16[512,1024]{1,0:T(8,128)(2,1)S(1)}, bf16[512,1024]{1,0:T(8,128)(2,1)}, u32[]{:S(2)}) copy-start(bf16[512,1024]{1,0:T(8,128)(2,1)} %amp_hbm.1) | copy-start | bytes 3145732
  2.5 1.0 %copy-start.1 = (f32[512,256]{1,0:T(8,128)S(1)}, f32[512,256]{1,0:T(8,128)}, u32[]{:S(2)}) copy-start(f32[512,256]{1,0:T(8,128)} %res_hbm.1) | copy-start | bytes 1572868
  3.6 0.9 %copy-start.2 = (bf16[512,256]{1,0:T(8,128)(2,1)S(1)}, bf16[512,256]{1,0:T(8,128)(2,1)}, u32[]{:S(2)}) copy-start(bf16[512,256]{1,0:T(8,128)(2,1)} %exch_hbm.1) | copy-start | bytes 786436
  4.5 0.8 %copy-start.3 = (bf16[128,256]{1,0:T(8,128)(2,1)S(1)}, bf16[128,256]{1,0:T(8,128)(2,1)}, u32[]{:S(2)}) copy-start(bf16[128,256]{1,0:T(8,128)(2,1)} %int_hbm.1) | copy-start | bytes 196612
  5.4 0.7 %copy-start.4 = (s32[8,8]{1,0:T(8,128)S(1)}, s32[8,8]{1,0:T(8,128)}, u32[]{:S(2)}) copy-start(s32[8,8]{1,0:T(8,128)} %amap_hbm.1) | copy-start | bytes 772

commit v2 on v1

--- a/solution.py
+++ b/solution.py
@@ -29,7 +29,7 @@
     n, nv,
     amp_hbm, amap_hbm, int_hbm, imap_hbm, exch_hbm, res_hbm,
     out_ref, energy_ref,
-    amp, amap, panel, imap, exch, acc, slots,
+    amp, amap, panel, screened, imap, exch, acc, slots,
     in_sem, core_send, core_recv, chip_send, chip_recv, en_send, en_recv,
 ):
     me = lax.axis_index("occ")
@@ -51,8 +51,6 @@
         pltpu.make_async_copy(res_hbm, acc, in_sem.at[4]),
         pltpu.make_async_copy(exch_hbm, exch, in_sem.at[5]),
     ]
-    for load in loads:
-        load.start()
 
     partners = [flipped(chip, s) for s in range(chips)]
     barrier = pltpu.get_barrier_semaphore()
@@ -62,32 +60,21 @@
     for s in range(1, nv):
         pl.semaphore_signal(barrier, inc=1, device_id=(me, lax.rem(mv + s, nv)), device_id_type=MESH)
 
-    loads[0].wait()
-    loads[1].wait()
-    grain = min(depth, VTILE)
-    while depth % grain or VTILE % grain:
-        grain //= 2
-    for t in range(depth // grain):
-        tile = (me * depth + t * grain) // VTILE
-        here = pl.ds(pl.multiple_of(me * depth + t * grain, grain), grain)
-        for c in range(cols // VTILE):
-            wide = pl.ds(c * VTILE, VTILE)
-            keep = imap[c, tile].astype(jnp.float32).astype(jnp.bfloat16)
-            panel[here, wide] = panel[here, wide] * keep
-
+    for load in loads:
+        load.start()
     pl.semaphore_wait(barrier, chips + nv - 1)
 
     def to_mate(s):
         owner = partners[s] * 2 + core
         return pltpu.make_async_remote_copy(
-            src_ref=block(owner), dst_ref=block(owner),
+            src_ref=block(owner) if s else int_hbm, dst_ref=block(owner),
             send_sem=core_send.at[s], recv_sem=core_recv.at[s],
             device_id=(mate, mv), device_id_type=MESH,
         )
 
     def to_chip(s):
         return pltpu.make_async_remote_copy(
-            src_ref=block(me), dst_ref=block(me),
+            src_ref=int_hbm, dst_ref=block(me),
             send_sem=chip_send.at[s], recv_sem=chip_recv.at[s],
             device_id=(partners[s] * 2 + core, mv), device_id_type=MESH,
         )
@@ -125,12 +112,24 @@
     loads[4].wait()
     loads[5].wait()
 
+    loads[0].wait()
+    loads[1].wait()
+    span = 2 * depth
+    grain = min(span, VTILE)
+    while span % grain or VTILE % grain:
+        grain //= 2
+
     def product(s):
-        span = 2 * depth
         start = partners[s] * span
+        for t in range(span // grain):
+            tile = (start + t * grain) // VTILE
+            here = pl.ds(pl.multiple_of(start + t * grain, grain), grain)
+            for c in range(cols // VTILE):
+                wide = pl.ds(c * VTILE, VTILE)
+                keep = imap[c, tile].astype(jnp.float32).astype(jnp.bfloat16)
+                screened[pl.ds(t * grain, grain), wide] = panel[here, wide] * keep
         return jnp.dot(
-            amp[:, pl.ds(pl.multiple_of(start, LANES), span)],
-            panel[pl.ds(pl.multiple_of(start, LANES), span), :],
+            amp[:, pl.ds(pl.multiple_of(start, LANES), span)], screened[...],
             preferred_element_type=jnp.float32,
         )
 
@@ -185,6 +184,17 @@
         mate_copies[s].wait_send()
 
 
+def deliver(residual, energy, residual_out, energy_out, sem):
+    copies = [
+        pltpu.make_async_copy(residual, residual_out, sem.at[0]),
+        pltpu.make_async_copy(energy, energy_out, sem.at[1]),
+    ]
+    for copy in copies:
+        copy.start()
+    for copy in copies:
+        copy.wait()
+
+
 def solution(mesh):
     n, nv = mesh.shape["occ"], mesh.shape["virt"]
     chips = n // 2
@@ -199,8 +209,8 @@
         residual, energy = pl.pallas_call(
             functools.partial(kernel, n, nv),
             out_shape=(
-                jax.ShapeDtypeStruct((rows, cols), jnp.float32),
-                jax.ShapeDtypeStruct((rows // LANES, LANES), jnp.float32),
+                pltpu.VMEM((rows, cols), jnp.float32),
+                pltpu.VMEM((rows // LANES, LANES), jnp.float32),
             ),
             in_specs=[hbm] * 6,
             out_specs=(vmem, vmem),
@@ -208,6 +218,7 @@
                 pltpu.VMEM((rows, k), jnp.bfloat16),
                 pltpu.SMEM(amp_map.shape, jnp.int32),
                 pltpu.VMEM((k, cols), jnp.bfloat16),
+                pltpu.VMEM((2 * depth, cols), jnp.bfloat16),
                 pltpu.SMEM(imap.shape, jnp.int32),
                 pltpu.VMEM((rows, cols), jnp.bfloat16),
                 pltpu.VMEM((rows, cols), jnp.float32),
@@ -224,7 +235,17 @@
                 collective_id=0, has_side_effects=True, vmem_limit_bytes=held + (8 << 20)
             ),
             cost_estimate=pl.CostEstimate(flops=2 * rows * k * cols, bytes_accessed=held, transcendentals=0),
-        )(amplitudes, amp_map, integrals, imap, exchange, residual_in)
+        )(*(pltpu.with_memory_space_constraint(x, pltpu.HBM) for x in (amplitudes, amp_map, integrals, imap, exchange, residual_in)))
+        residual, energy = pl.pallas_call(
+            deliver,
+            out_shape=(
+                jax.ShapeDtypeStruct((rows, cols), jnp.float32),
+                jax.ShapeDtypeStruct((rows // LANES, LANES), jnp.float32),
+            ),
+            in_specs=[vmem, vmem],
+            out_specs=(hbm, hbm),
+            scratch_shapes=[pltpu.SemaphoreType.DMA((2,))],
+        )(residual, energy)
         return residual, energy.reshape(rows)
 
     in_specs = (

time: 22.9 us -> 19.3 us (0.84)
  local copies, waits for them, and re-layouts: 6.79 us -> 1.38 us
  Pallas kernels: 15.2 us -> 17.1 us
    unnamed x14 -> x4, local copies, waits for them, and re-layouts: 6.79 us -> 1.38 us
    pallas_call x1 -> x2, Pallas kernels: 15.2 us -> 17.1 us  [the longest x1 15.3 us: on_device(): pl.pallas_call(functools.partial(kernel, n, nv), out_shape=(pltpu.VMEM((r...]
where the time goes in v2:
time: 19.3 us; the launch traced here: 19.2 us
  Pallas kernels  17.1 us (89%)
  local copies, waits for them, and re-layouts  1.38 us (7%)
  between operations  0.65 us (3%)
    pallas_call x1, Pallas kernels, on_device(): pl.pallas_call(functools.partial(kernel, n, nv), out_shape=(pltpu.VMEM((r...  15.3 us
    pallas_call x1, Pallas kernels, on_device(): pl.pallas_call(deliver, out_shape=(jax.ShapeDtypeStruct((rows, cols), jnp...  1.85 us
    unnamed x4, local copies, waits for them, and re-layouts  1.38 us

profile of v2, /device:TPU:0, one launch (start us, length us, event | category | flops | bytes accessed | tf_op | source)
XLA Modules:
  0.0 19.2 jit_solution(6107444144179383860)
XLA Ops:
  0.6 15.3 %shard_map.77 = (f32[512,256]{1,0:T(8,128)S(1)}, f32[4,128]{1,0:T(4,128)S(1)}) custom-call(bf16[512,1024]{1,0:T(8,128)(2,1)} %amp_hbm.1, s32[8,8]{1,0:T(8,128)} %amap_hbm.1, bf16[128,256]{1,0:T(8,128)(2,1)} %int_hbm.1, s32[2,8]{1,0:T(2,128)} %bitcast.2, bf16[512,256]{1,0:T(8,128)(2,1)} %exch_hbm.1, f32[512,256]{1,0:T(8,128)} %res_hbm.1), custom_call_target="tpu_custom_call" | custom-call | flops 268435456 | bytes 2883584 | tf_op jit(solution)/shard_map/pallas_call | solution.py:209
  15.9 0.0 copy-start
  15.9 0.8 %copy-done = f32[512,256]{1,0:T(8,128)} copy-done((f32[512,256]{1,0:T(8,128)}, f32[512,256]{1,0:T(8,128)S(1)}, u32[]{:S(2)}) %copy-start) | copy-done | bytes 524312
  16.7 0.0 copy-start.1
  16.7 0.6 %copy-done.1 = f32[4,128]{1,0:T(4,128)} copy-done((f32[4,128]{1,0:T(4,128)}, f32[4,128]{1,0:T(4,128)S(1)}, u32[]{:S(2)}) %copy-start.1) | copy-done | bytes 2072
  17.3 1.9 %shard_map.78 = (f32[512,256]{1,0:T(8,128)}, f32[4,128]{1,0:T(4,128)}) custom-call(f32[512,256]{1,0:T(8,128)} %copy-done, f32[4,128]{1,0:T(4,128)} %copy-done.1), custom_call_target="tpu_custom_call" | custom-call | tf_op jit(solution)/shard_map/pallas_call | solution.py:239
Async XLA Ops:
  15.9 0.8 %copy-start = (f32[512,256]{1,0:T(8,128)}, f32[512,256]{1,0:T(8,128)S(1)}, u32[]{:S(2)}) copy-start(f32[512,256]{1,0:T(8,128)S(1)} %get-tuple-element.6.residual) | copy-start | bytes 1572868
  16.7 0.6 %copy-start.1 = (f32[4,128]{1,0:T(4,128)}, f32[4,128]{1,0:T(4,128)S(1)}, u32[]{:S(2)}) copy-start(f32[4,128]{1,0:T(4,128)S(1)} %get-tuple-element.7.energy) | copy-start | bytes 6148

commit v3 on v2

--- a/solution.py
+++ b/solution.py
@@ -60,8 +60,6 @@
     for s in range(1, nv):
         pl.semaphore_signal(barrier, inc=1, device_id=(me, lax.rem(mv + s, nv)), device_id_type=MESH)
 
-    for load in loads:
-        load.start()
     pl.semaphore_wait(barrier, chips + nv - 1)
 
     def to_mate(s):
@@ -100,6 +98,8 @@
     for s in range(1, chips):
         chip_copies[s].start()
     mate_copies[0].start()
+    for load in loads:
+        load.start()
 
     loads[2].wait()
     loads[3].wait()
@@ -245,7 +245,7 @@
             in_specs=[vmem, vmem],
             out_specs=(hbm, hbm),
             scratch_shapes=[pltpu.SemaphoreType.DMA((2,))],
-        )(residual, energy)
+        )(*(pltpu.with_memory_space_constraint(x, pltpu.VMEM) for x in (residual, energy)))
         return residual, energy.reshape(rows)
 
     in_specs = (

time: 19.3 us -> 16.9 us (0.88)
  local copies, waits for them, and re-layouts: 1.38 us -> 0 us
  Pallas kernels: 17.1 us -> 16.1 us
    unnamed x4 -> x0, local copies, waits for them, and re-layouts: 1.38 us -> none
    pallas_call x1, Pallas kernels: 1.85 us -> 0.81 us  [on_device(): pl.pallas_call(deliver, out_shape=(jax.ShapeDtypeStruct((rows, cols), jnp...]
where the time goes in v3:
time: 16.9 us; the launch traced here: 16.7 us
  Pallas kernels  16.1 us (95%)
  between operations  0.64 us (4%)
    pallas_call x1, Pallas kernels, on_device(): pl.pallas_call(functools.partial(kernel, n, nv), out_shape=(pltpu.VMEM((r...  15.3 us
    pallas_call x1, Pallas kernels, on_device(): pl.pallas_call(deliver, out_shape=(jax.ShapeDtypeStruct((rows, cols), jnp...  0.81 us

profile of v3, /device:TPU:0, one launch (start us, length us, event | category | flops | bytes accessed | tf_op | source)
XLA Modules:
  0.0 16.7 jit_solution(6083843823415914960)
XLA Ops:
  0.6 15.3 %shard_map.77 = (f32[512,256]{1,0:T(8,128)S(1)}, f32[4,128]{1,0:T(4,128)S(1)}) custom-call(bf16[512,1024]{1,0:T(8,128)(2,1)} %amp_hbm.1, s32[8,8]{1,0:T(8,128)} %amap_hbm.1, bf16[128,256]{1,0:T(8,128)(2,1)} %int_hbm.1, s32[2,8]{1,0:T(2,128)} %bitcast.2, bf16[512,256]{1,0:T(8,128)(2,1)} %exch_hbm.1, f32[512,256]{1,0:T(8,128)} %res_hbm.1), custom_call_target="tpu_custom_call" | custom-call | flops 268435456 | bytes 2883584 | tf_op jit(solution)/shard_map/pallas_call | solution.py:209
  15.9 0.8 %shard_map.78 = (f32[512,256]{1,0:T(8,128)}, f32[4,128]{1,0:T(4,128)}) custom-call(f32[512,256]{1,0:T(8,128)S(1)} %get-tuple-element.6.residual, f32[4,128]{1,0:T(4,128)S(1)} %get-tuple-element.7.energy), custom_call_target="tpu_custom_call" | custom-call | tf_op jit(solution)/shard_map/pallas_call | solution.py:239

commit v4 on v3

--- a/solution.py
+++ b/solution.py
@@ -55,51 +55,68 @@
     partners = [flipped(chip, s) for s in range(chips)]
     barrier = pltpu.get_barrier_semaphore()
     pl.semaphore_signal(barrier, inc=1, device_id=(mate, mv), device_id_type=MESH)
-    for s in range(1, chips):
+    relayed = chips == 4
+    greeted = (1, 2) if relayed else tuple(range(1, chips))
+    for s in greeted:
         pl.semaphore_signal(barrier, inc=1, device_id=(partners[s] * 2 + core, mv), device_id_type=MESH)
     for s in range(1, nv):
         pl.semaphore_signal(barrier, inc=1, device_id=(me, lax.rem(mv + s, nv)), device_id_type=MESH)
 
-    pl.semaphore_wait(barrier, chips + nv - 1)
-
-    def to_mate(s):
-        owner = partners[s] * 2 + core
+    pl.semaphore_wait(barrier, len(greeted) + nv)
+
+    def push(owner, part, target, send, recv):
+        low, size = part
+        here = panel.at[pl.ds(pl.multiple_of(owner * depth + low, 16), size), :]
+        source = int_hbm.at[pl.ds(low, size), :] if owner is me else here
         return pltpu.make_async_remote_copy(
-            src_ref=block(owner) if s else int_hbm, dst_ref=block(owner),
-            send_sem=core_send.at[s], recv_sem=core_recv.at[s],
-            device_id=(mate, mv), device_id_type=MESH,
+            src_ref=source, dst_ref=here, send_sem=send, recv_sem=recv,
+            device_id=(target, mv), device_id_type=MESH,
         )
 
-    def to_chip(s):
-        return pltpu.make_async_remote_copy(
-            src_ref=int_hbm, dst_ref=block(me),
-            send_sem=chip_send.at[s], recv_sem=chip_recv.at[s],
-            device_id=(partners[s] * 2 + core, mv), device_id_type=MESH,
-        )
-
-    def from_chip(s):
-        owner = partners[s] * 2 + core
-        return pltpu.make_async_remote_copy(
-            src_ref=block(owner), dst_ref=block(owner),
-            send_sem=chip_send.at[s], recv_sem=chip_recv.at[s],
-            device_id=(partners[s] * 2 + core, mv), device_id_type=MESH,
-        )
-
-    def from_mate(s):
-        owner = partners[s] * 2 + (1 - core)
-        return pltpu.make_async_remote_copy(
-            src_ref=block(owner), dst_ref=block(owner),
-            send_sem=core_send.at[s], recv_sem=core_recv.at[s],
-            device_id=(mate, mv), device_id_type=MESH,
-        )
-
-    chip_copies = [None] + [to_chip(s) for s in range(1, chips)]
-    mate_copies = [to_mate(s) for s in range(chips)]
-    for s in range(1, chips):
-        chip_copies[s].start()
-    mate_copies[0].start()
+    full, top, bottom = (0, depth), (0, depth // 2), (depth // 2, depth - depth // 2)
+    theirs = [p * 2 + core for p in partners]
+    theirs[0] = me
+    others = [p * 2 + (1 - core) for p in partners]
+
+    def to_mate(s, part=full, k=0):
+        return push(theirs[s], part, mate, core_send.at[s, k], core_recv.at[s, k])
+
+    def from_mate(s, part=full, k=0):
+        return push(others[s], part, mate, core_send.at[s, k], core_recv.at[s, k])
+
+    def to_chip(s, part=full, k=0):
+        return push(me, part, theirs[s], chip_send.at[s, k], chip_recv.at[s, k])
+
+    def from_chip(s, part=full, k=0):
+        return push(theirs[s], part, theirs[s], chip_send.at[s, k], chip_recv.at[s, k])
+
+    sent = []
+
+    def go(copy):
+        copy.start()
+        sent.append(copy)
+
+    if relayed:
+        go(to_chip(1, top, 0))
+        go(to_chip(2, bottom, 1))
+        go(to_chip(1, bottom, 1))
+        go(to_chip(2, top, 0))
+    else:
+        for s in range(1, chips):
+            go(to_chip(s))
+    go(to_mate(0))
     for load in loads:
         load.start()
+
+    if relayed:
+        from_chip(1, top, 0).wait_recv()
+        go(push(theirs[1], top, theirs[2], chip_send.at[3, 0], chip_recv.at[3, 0]))
+        from_chip(2, bottom, 1).wait_recv()
+        go(push(theirs[2], bottom, theirs[1], chip_send.at[3, 1], chip_recv.at[3, 1]))
+        from_chip(1, bottom, 1).wait_recv()
+        go(to_mate(1))
+        from_chip(2, top, 0).wait_recv()
+        go(to_mate(2))
 
     loads[2].wait()
     loads[3].wait()
@@ -133,17 +150,30 @@
             preferred_element_type=jnp.float32,
         )
 
-    for s in range(chips):
-        if s + 1 < chips:
-            if s == 0:
-                from_mate(0).wait_recv()
-                acc[...] += product(0)
-            from_chip(s + 1).wait_recv()
-            mate_copies[s + 1].start()
-        if s > 0:
+    if relayed:
+        from_mate(0).wait_recv()
+        acc[...] += product(0)
+        push(theirs[3], top, theirs[2], chip_send.at[3, 0], chip_recv.at[3, 0]).wait_recv()
+        go(to_mate(3, top, 0))
+        push(theirs[3], bottom, theirs[1], chip_send.at[3, 1], chip_recv.at[3, 1]).wait_recv()
+        go(to_mate(3, bottom, 1))
+        for s in (1, 2):
             from_mate(s).wait_recv()
-            if s < chips - 1:
-                acc[...] += product(s)
+            acc[...] += product(s)
+        from_mate(3, top, 0).wait_recv()
+        from_mate(3, bottom, 1).wait_recv()
+    else:
+        from_mate(0).wait_recv()
+        if chips > 1:
+            acc[...] += product(0)
+        for s in range(1, chips):
+            from_chip(s).wait_recv()
+            go(to_mate(s))
+            if s > 1:
+                from_mate(s - 1).wait_recv()
+                acc[...] += product(s - 1)
+        if chips > 1:
+            from_mate(chips - 1).wait_recv()
 
     residual = acc[...] + product(chips - 1)
     out_ref[...] = residual
@@ -155,15 +185,12 @@
         part = folded[q * LANES:(q + 1) * LANES, :].T
         slots[mv, pl.ds(q, 1), :] = jnp.sum(part, axis=0, keepdims=True)
 
-    sends = []
     for s in range(1, nv):
-        send = pltpu.make_async_remote_copy(
+        go(pltpu.make_async_remote_copy(
             src_ref=slots.at[mv], dst_ref=slots.at[mv],
             send_sem=en_send.at[s], recv_sem=en_recv.at[s],
             device_id=(me, lax.rem(mv + s, nv)), device_id_type=MESH,
-        )
-        send.start()
-        sends.append(send)
+        ))
     for s in range(1, nv):
         origin = lax.rem(mv + nv - s, nv)
         pltpu.make_async_remote_copy(
@@ -176,12 +203,8 @@
         total = total + slots[v]
     energy_ref[...] = total
 
-    for send in sends:
-        send.wait_send()
-    for s in range(1, chips):
-        chip_copies[s].wait_send()
-    for s in range(chips):
-        mate_copies[s].wait_send()
+    for copy in sent:
+        copy.wait_send()
 
 
 def deliver(residual, energy, residual_out, energy_out, sem):
@@ -224,10 +247,10 @@
                 pltpu.VMEM((rows, cols), jnp.float32),
                 pltpu.VMEM((nv, rows // LANES, LANES), jnp.float32),
                 pltpu.SemaphoreType.DMA((6,)),
-                pltpu.SemaphoreType.DMA((chips,)),
-                pltpu.SemaphoreType.DMA((chips,)),
-                pltpu.SemaphoreType.DMA((chips,)),
-                pltpu.SemaphoreType.DMA((chips,)),
+                pltpu.SemaphoreType.DMA((chips, 2)),
+                pltpu.SemaphoreType.DMA((chips, 2)),
+                pltpu.SemaphoreType.DMA((chips, 2)),
+                pltpu.SemaphoreType.DMA((chips, 2)),
                 pltpu.SemaphoreType.DMA((nv,)),
                 pltpu.SemaphoreType.DMA((nv,)),
             ],

time: 16.9 us -> 17.2 us (1.018)
  Pallas kernels: 16.1 us -> 16.5 us
    pallas_call x1, Pallas kernels: 15.3 us -> 15.6 us  [on_device(): pl.pallas_call(functools.partial(kernel, n, nv), out_shape=(pltpu.VMEM((r...]
where the time goes in v4:
time: 17.2 us; the launch traced here: 17.1 us
  Pallas kernels  16.5 us (96%)
  between operations  0.64 us (4%)
    pallas_call x1, Pallas kernels, on_device(): pl.pallas_call(functools.partial(kernel, n, nv), out_shape=(pltpu.VMEM((r...  15.6 us
    pallas_call x1, Pallas kernels, on_device(): pl.pallas_call(deliver, out_shape=(jax.ShapeDtypeStruct((rows, cols), jnp...  0.81 us

profile of v4, /device:TPU:0, one launch (start us, length us, event | category | flops | bytes accessed | tf_op | source)
XLA Modules:
  0.0 17.1 jit_solution(10700945877607596001)
XLA Ops:
  0.6 15.6 %shard_map.77 = (f32[512,256]{1,0:T(8,128)S(1)}, f32[4,128]{1,0:T(4,128)S(1)}) custom-call(bf16[512,1024]{1,0:T(8,128)(2,1)} %amp_hbm.1, s32[8,8]{1,0:T(8,128)} %amap_hbm.1, bf16[128,256]{1,0:T(8,128)(2,1)} %int_hbm.1, s32[2,8]{1,0:T(2,128)} %bitcast.2, bf16[512,256]{1,0:T(8,128)(2,1)} %exch_hbm.1, f32[512,256]{1,0:T(8,128)} %res_hbm.1), custom_call_target="tpu_custom_call" | custom-call | flops 268435456 | bytes 2883584 | tf_op jit(solution)/shard_map/pallas_call | solution.py:232
  16.3 0.8 %shard_map.78 = (f32[512,256]{1,0:T(8,128)}, f32[4,128]{1,0:T(4,128)}) custom-call(f32[512,256]{1,0:T(8,128)S(1)} %get-tuple-element.6.residual, f32[4,128]{1,0:T(4,128)S(1)} %get-tuple-element.7.energy), custom_call_target="tpu_custom_call" | custom-call | tf_op jit(solution)/shard_map/pallas_call | solution.py:262

commit v5 on v3

--- a/solution.py
+++ b/solution.py
@@ -62,42 +62,37 @@
 
     pl.semaphore_wait(barrier, chips + nv - 1)
 
+    def push(owner, target, send, recv):
+        return pltpu.make_async_remote_copy(
+            src_ref=int_hbm if owner is me else block(owner), dst_ref=block(owner),
+            send_sem=send, recv_sem=recv, device_id=(target, mv), device_id_type=MESH,
+        )
+
+    theirs = [p * 2 + core for p in partners]
+    theirs[0] = me
+    others = [p * 2 + (1 - core) for p in partners]
+
     def to_mate(s):
-        owner = partners[s] * 2 + core
-        return pltpu.make_async_remote_copy(
-            src_ref=block(owner) if s else int_hbm, dst_ref=block(owner),
-            send_sem=core_send.at[s], recv_sem=core_recv.at[s],
-            device_id=(mate, mv), device_id_type=MESH,
-        )
+        return push(theirs[s], mate, core_send.at[s], core_recv.at[s])
+
+    def from_mate(s):
+        return push(others[s], mate, core_send.at[s], core_recv.at[s])
 
     def to_chip(s):
-        return pltpu.make_async_remote_copy(
-            src_ref=int_hbm, dst_ref=block(me),
-            send_sem=chip_send.at[s], recv_sem=chip_recv.at[s],
-            device_id=(partners[s] * 2 + core, mv), device_id_type=MESH,
-        )
+        return push(me, theirs[s], chip_send.at[s], chip_recv.at[s])
 
     def from_chip(s):
-        owner = partners[s] * 2 + core
-        return pltpu.make_async_remote_copy(
-            src_ref=block(owner), dst_ref=block(owner),
-            send_sem=chip_send.at[s], recv_sem=chip_recv.at[s],
-            device_id=(partners[s] * 2 + core, mv), device_id_type=MESH,
-        )
-
-    def from_mate(s):
-        owner = partners[s] * 2 + (1 - core)
-        return pltpu.make_async_remote_copy(
-            src_ref=block(owner), dst_ref=block(owner),
-            send_sem=core_send.at[s], recv_sem=core_recv.at[s],
-            device_id=(mate, mv), device_id_type=MESH,
-        )
-
-    chip_copies = [None] + [to_chip(s) for s in range(1, chips)]
-    mate_copies = [to_mate(s) for s in range(chips)]
-    for s in range(1, chips):
-        chip_copies[s].start()
-    mate_copies[0].start()
+        return push(theirs[s], theirs[s], chip_send.at[s], chip_recv.at[s])
+
+    sent = []
+
+    def go(copy):
+        copy.start()
+        sent.append(copy)
+
+    for s in reversed(range(1, chips)):
+        go(to_chip(s))
+    go(to_mate(0))
     for load in loads:
         load.start()
 
@@ -133,17 +128,13 @@
             preferred_element_type=jnp.float32,
         )
 
+    for s in range(1, chips):
+        from_chip(s).wait_recv()
+        go(to_mate(s))
     for s in range(chips):
-        if s + 1 < chips:
-            if s == 0:
-                from_mate(0).wait_recv()
-                acc[...] += product(0)
-            from_chip(s + 1).wait_recv()
-            mate_copies[s + 1].start()
-        if s > 0:
-            from_mate(s).wait_recv()
-            if s < chips - 1:
-                acc[...] += product(s)
+        from_mate(s).wait_recv()
+        if s < chips - 1:
+            acc[...] += product(s)
 
     residual = acc[...] + product(chips - 1)
     out_ref[...] = residual
@@ -155,15 +146,12 @@
         part = folded[q * LANES:(q + 1) * LANES, :].T
         slots[mv, pl.ds(q, 1), :] = jnp.sum(part, axis=0, keepdims=True)
 
-    sends = []
     for s in range(1, nv):
-        send = pltpu.make_async_remote_copy(
+        go(pltpu.make_async_remote_copy(
             src_ref=slots.at[mv], dst_ref=slots.at[mv],
             send_sem=en_send.at[s], recv_sem=en_recv.at[s],
             device_id=(me, lax.rem(mv + s, nv)), device_id_type=MESH,
-        )
-        send.start()
-        sends.append(send)
+        ))
     for s in range(1, nv):
         origin = lax.rem(mv + nv - s, nv)
         pltpu.make_async_remote_copy(
@@ -176,12 +164,8 @@
         total = total + slots[v]
     energy_ref[...] = total
 
-    for send in sends:
-        send.wait_send()
-    for s in range(1, chips):
-        chip_copies[s].wait_send()
-    for s in range(chips):
-        mate_copies[s].wait_send()
+    for copy in sent:
+        copy.wait_send()
 
 
 def deliver(residual, energy, residual_out, energy_out, sem):

time: 16.9 us -> 16.2 us (0.959)
  Pallas kernels: 16.1 us -> 15.5 us
    pallas_call x1, Pallas kernels: 15.3 us -> 14.6 us  [on_device(): pl.pallas_call(functools.partial(kernel, n, nv), out_shape=(pltpu.VMEM((r...]
where the time goes in v5:
time: 16.2 us; the launch traced here: 16.1 us
  Pallas kernels  15.5 us (96%)
  between operations  0.64 us (4%)
    pallas_call x1, Pallas kernels, on_device(): pl.pallas_call(functools.partial(kernel, n, nv), out_shape=(pltpu.VMEM((r...  14.6 us
    pallas_call x1, Pallas kernels, on_device(): pl.pallas_call(deliver, out_shape=(jax.ShapeDtypeStruct((rows, cols), jnp...  0.81 us

profile of v5, /device:TPU:0, one launch (start us, length us, event | category | flops | bytes accessed | tf_op | source)
XLA Modules:
  0.0 16.1 jit_solution(5061261122806237472)
XLA Ops:
  0.6 14.6 %shard_map.77 = (f32[512,256]{1,0:T(8,128)S(1)}, f32[4,128]{1,0:T(4,128)S(1)}) custom-call(bf16[512,1024]{1,0:T(8,128)(2,1)} %amp_hbm.1, s32[8,8]{1,0:T(8,128)} %amap_hbm.1, bf16[128,256]{1,0:T(8,128)(2,1)} %int_hbm.1, s32[2,8]{1,0:T(2,128)} %bitcast.2, bf16[512,256]{1,0:T(8,128)(2,1)} %exch_hbm.1, f32[512,256]{1,0:T(8,128)} %res_hbm.1), custom_call_target="tpu_custom_call" | custom-call | flops 268435456 | bytes 2883584 | tf_op jit(solution)/shard_map/pallas_call | solution.py:193
  15.3 0.8 %shard_map.78 = (f32[512,256]{1,0:T(8,128)}, f32[4,128]{1,0:T(4,128)}) custom-call(f32[512,256]{1,0:T(8,128)S(1)} %get-tuple-element.6.residual, f32[4,128]{1,0:T(4,128)S(1)} %get-tuple-element.7.energy), custom_call_target="tpu_custom_call" | custom-call | tf_op jit(solution)/shard_map/pallas_call | solution.py:223

commit v6 on v5

--- a/solution.py
+++ b/solution.py
@@ -10,6 +10,7 @@
 PTILE = 64
 VTILE = 128
 LANES = 128
+PARTS = 4
 MESH = pl.DeviceIdType.MESH
 
 
@@ -54,17 +55,19 @@
 
     partners = [flipped(chip, s) for s in range(chips)]
     barrier = pltpu.get_barrier_semaphore()
+    for s in reversed(range(1, chips)):
+        pl.semaphore_signal(barrier, inc=1, device_id=(partners[s] * 2 + core, mv), device_id_type=MESH)
     pl.semaphore_signal(barrier, inc=1, device_id=(mate, mv), device_id_type=MESH)
-    for s in range(1, chips):
-        pl.semaphore_signal(barrier, inc=1, device_id=(partners[s] * 2 + core, mv), device_id_type=MESH)
     for s in range(1, nv):
         pl.semaphore_signal(barrier, inc=1, device_id=(me, lax.rem(mv + s, nv)), device_id_type=MESH)
-
+    for load in loads:
+        load.start()
+    loads[0].wait()
     pl.semaphore_wait(barrier, chips + nv - 1)
 
     def push(owner, target, send, recv):
         return pltpu.make_async_remote_copy(
-            src_ref=int_hbm if owner is me else block(owner), dst_ref=block(owner),
+            src_ref=block(owner), dst_ref=block(owner),
             send_sem=send, recv_sem=recv, device_id=(target, mv), device_id_type=MESH,
         )
 
@@ -93,8 +96,6 @@
     for s in reversed(range(1, chips)):
         go(to_chip(s))
     go(to_mate(0))
-    for load in loads:
-        load.start()
 
     loads[2].wait()
     loads[3].wait()
@@ -106,8 +107,6 @@
             amp[tall, wide] = amp[tall, wide] * keep
     loads[4].wait()
     loads[5].wait()
-
-    loads[0].wait()
     loads[1].wait()
     span = 2 * depth
     grain = min(span, VTILE)
@@ -169,10 +168,11 @@
 
 
 def deliver(residual, energy, residual_out, energy_out, sem):
-    copies = [
-        pltpu.make_async_copy(residual, residual_out, sem.at[0]),
-        pltpu.make_async_copy(energy, energy_out, sem.at[1]),
-    ]
+    part = residual.shape[0] // PARTS
+    copies = [pltpu.make_async_copy(energy, energy_out, sem.at[PARTS])]
+    for p in range(PARTS):
+        here = pl.ds(p * part, part)
+        copies.append(pltpu.make_async_copy(residual.at[here, :], residual_out.at[here, :], sem.at[p]))
     for copy in copies:
         copy.start()
     for copy in copies:
@@ -228,7 +228,7 @@
             ),
             in_specs=[vmem, vmem],
             out_specs=(hbm, hbm),
-            scratch_shapes=[pltpu.SemaphoreType.DMA((2,))],
+            scratch_shapes=[pltpu.SemaphoreType.DMA((PARTS + 1,))],
         )(*(pltpu.with_memory_space_constraint(x, pltpu.VMEM) for x in (residual, energy)))
         return residual, energy.reshape(rows)
 

time: 16.2 us -> 16 us (0.988)
  Pallas kernels: 15.5 us -> 15.2 us
    pallas_call x1, Pallas kernels: 14.6 us -> 14.4 us  [on_device(): pl.pallas_call(functools.partial(kernel, n, nv), out_shape=(pltpu.VMEM((r...]
where the time goes in v6:
time: 16 us; the launch traced here: 15.9 us
  Pallas kernels  15.2 us (95%)
  between operations  0.64 us (4%)
    pallas_call x1, Pallas kernels, on_device(): pl.pallas_call(functools.partial(kernel, n, nv), out_shape=(pltpu.VMEM((r...  14.4 us
    pallas_call x1, Pallas kernels, on_device(): pl.pallas_call(deliver, out_shape=(jax.ShapeDtypeStruct((rows, cols), jnp...  0.83 us

profile of v6, /device:TPU:0, one launch (start us, length us, event | category | flops | bytes accessed | tf_op | source)
XLA Modules:
  0.0 15.9 jit_solution(9145409284876118496)
XLA Ops:
  0.6 14.4 %shard_map.77 = (f32[512,256]{1,0:T(8,128)S(1)}, f32[4,128]{1,0:T(4,128)S(1)}) custom-call(bf16[512,1024]{1,0:T(8,128)(2,1)} %amp_hbm.1, s32[8,8]{1,0:T(8,128)} %amap_hbm.1, bf16[128,256]{1,0:T(8,128)(2,1)} %int_hbm.1, s32[2,8]{1,0:T(2,128)} %bitcast.2, bf16[512,256]{1,0:T(8,128)(2,1)} %exch_hbm.1, f32[512,256]{1,0:T(8,128)} %res_hbm.1), custom_call_target="tpu_custom_call" | custom-call | flops 268435456 | bytes 2883584 | tf_op jit(solution)/shard_map/pallas_call | solution.py:193
  15.0 0.8 %shard_map.78 = (f32[512,256]{1,0:T(8,128)}, f32[4,128]{1,0:T(4,128)}) custom-call(f32[512,256]{1,0:T(8,128)S(1)} %get-tuple-element.6.residual, f32[4,128]{1,0:T(4,128)S(1)} %get-tuple-element.7.energy), custom_call_target="tpu_custom_call" | custom-call | tf_op jit(solution)/shard_map/pallas_call | solution.py:223

commit v7 on v6

--- a/solution.py
+++ b/solution.py
@@ -31,13 +31,12 @@
     amp_hbm, amap_hbm, int_hbm, imap_hbm, exch_hbm, res_hbm,
     out_ref, energy_ref,
     amp, amap, panel, screened, imap, exch, acc, slots,
-    in_sem, core_send, core_recv, chip_send, chip_recv, en_send, en_recv,
+    in_sem, part_send, part_recv, en_send, en_recv,
 ):
     me = lax.axis_index("occ")
     mv = lax.axis_index("virt")
     chips = n // 2
     chip, core = me // 2, lax.rem(me, 2)
-    mate = chip * 2 + (1 - core)
     depth = int_hbm.shape[0]
     rows, cols = out_ref.shape
 
@@ -54,38 +53,23 @@
     ]
 
     partners = [flipped(chip, s) for s in range(chips)]
+    peers = [(partners[s] * 2 + c, 2 * s + f) for s in reversed(range(chips)) for f, c in enumerate((core, 1 - core)) if s or f]
     barrier = pltpu.get_barrier_semaphore()
-    for s in reversed(range(1, chips)):
-        pl.semaphore_signal(barrier, inc=1, device_id=(partners[s] * 2 + core, mv), device_id_type=MESH)
-    pl.semaphore_signal(barrier, inc=1, device_id=(mate, mv), device_id_type=MESH)
+    for owner, _ in peers:
+        pl.semaphore_signal(barrier, inc=1, device_id=(owner, mv), device_id_type=MESH)
     for s in range(1, nv):
         pl.semaphore_signal(barrier, inc=1, device_id=(me, lax.rem(mv + s, nv)), device_id_type=MESH)
     for load in loads:
         load.start()
     loads[0].wait()
-    pl.semaphore_wait(barrier, chips + nv - 1)
-
-    def push(owner, target, send, recv):
+    pl.semaphore_wait(barrier, n + nv - 2)
+
+    def push(owner, target, slot):
         return pltpu.make_async_remote_copy(
             src_ref=block(owner), dst_ref=block(owner),
-            send_sem=send, recv_sem=recv, device_id=(target, mv), device_id_type=MESH,
+            send_sem=part_send.at[slot], recv_sem=part_recv.at[slot],
+            device_id=(target, mv), device_id_type=MESH,
         )
-
-    theirs = [p * 2 + core for p in partners]
-    theirs[0] = me
-    others = [p * 2 + (1 - core) for p in partners]
-
-    def to_mate(s):
-        return push(theirs[s], mate, core_send.at[s], core_recv.at[s])
-
-    def from_mate(s):
-        return push(others[s], mate, core_send.at[s], core_recv.at[s])
-
-    def to_chip(s):
-        return push(me, theirs[s], chip_send.at[s], chip_recv.at[s])
-
-    def from_chip(s):
-        return push(theirs[s], theirs[s], chip_send.at[s], chip_recv.at[s])
 
     sent = []
 
@@ -93,9 +77,8 @@
         copy.start()
         sent.append(copy)
 
-    for s in reversed(range(1, chips)):
-        go(to_chip(s))
-    go(to_mate(0))
+    for target, slot in peers:
+        go(push(me, target, slot))
 
     loads[2].wait()
     loads[3].wait()
@@ -127,11 +110,10 @@
             preferred_element_type=jnp.float32,
         )
 
-    for s in range(1, chips):
-        from_chip(s).wait_recv()
-        go(to_mate(s))
     for s in range(chips):
-        from_mate(s).wait_recv()
+        for owner, slot in peers:
+            if slot // 2 == s:
+                push(owner, owner, slot).wait_recv()
         if s < chips - 1:
             acc[...] += product(s)
 
@@ -181,7 +163,6 @@
 
 def solution(mesh):
     n, nv = mesh.shape["occ"], mesh.shape["virt"]
-    chips = n // 2
 
     def on_device(amplitudes, amp_map, integrals, int_map, exchange, residual_in):
         rows, k = amplitudes.shape
@@ -208,10 +189,8 @@
                 pltpu.VMEM((rows, cols), jnp.float32),
                 pltpu.VMEM((nv, rows // LANES, LANES), jnp.float32),
                 pltpu.SemaphoreType.DMA((6,)),
-                pltpu.SemaphoreType.DMA((chips,)),
-                pltpu.SemaphoreType.DMA((chips,)),
-                pltpu.SemaphoreType.DMA((chips,)),
-                pltpu.SemaphoreType.DMA((chips,)),
+                pltpu.SemaphoreType.DMA((n,)),
+                pltpu.SemaphoreType.DMA((n,)),
                 pltpu.SemaphoreType.DMA((nv,)),
                 pltpu.SemaphoreType.DMA((nv,)),
             ],

time: 16 us -> 18.8 us (1.18)
  Pallas kernels: 15.2 us -> 18 us
    pallas_call x1, Pallas kernels: 14.4 us -> 17.2 us  [on_device(): pl.pallas_call(functools.partial(kernel, n, nv), out_shape=(pltpu.VMEM((r...]
where the time goes in v7:
time: 18.8 us; the launch traced here: 18.7 us
  Pallas kernels  18 us (96%)
  between operations  0.64 us (3%)
    pallas_call x1, Pallas kernels, on_device(): pl.pallas_call(functools.partial(kernel, n, nv), out_shape=(pltpu.VMEM((r...  17.2 us
    pallas_call x1, Pallas kernels, on_device(): pl.pallas_call(deliver, out_shape=(jax.ShapeDtypeStruct((rows, cols), jnp...  0.83 us

profile of v7, /device:TPU:0, one launch (start us, length us, event | category | flops | bytes accessed | tf_op | source)
XLA Modules:
  0.0 18.7 jit_solution(6142728458213171265)
XLA Ops:
  0.6 17.2 %shard_map.77 = (f32[512,256]{1,0:T(8,128)S(1)}, f32[4,128]{1,0:T(4,128)S(1)}) custom-call(bf16[512,1024]{1,0:T(8,128)(2,1)} %amp_hbm.1, s32[8,8]{1,0:T(8,128)} %amap_hbm.1, bf16[128,256]{1,0:T(8,128)(2,1)} %int_hbm.1, s32[2,8]{1,0:T(2,128)} %bitcast.2, bf16[512,256]{1,0:T(8,128)(2,1)} %exch_hbm.1, f32[512,256]{1,0:T(8,128)} %res_hbm.1), custom_call_target="tpu_custom_call" | custom-call | flops 268435456 | bytes 2883584 | tf_op jit(solution)/shard_map/pallas_call | solution.py:174
  17.8 0.8 %shard_map.78 = (f32[512,256]{1,0:T(8,128)}, f32[4,128]{1,0:T(4,128)}) custom-call(f32[512,256]{1,0:T(8,128)S(1)} %get-tuple-element.6.residual, f32[4,128]{1,0:T(4,128)S(1)} %get-tuple-element.7.energy), custom_call_target="tpu_custom_call" | custom-call | tf_op jit(solution)/shard_map/pallas_call | solution.py:202

commit v8 on v4

--- a/solution.py
+++ b/solution.py
@@ -54,22 +54,23 @@
 
     partners = [flipped(chip, s) for s in range(chips)]
     barrier = pltpu.get_barrier_semaphore()
-    pl.semaphore_signal(barrier, inc=1, device_id=(mate, mv), device_id_type=MESH)
     relayed = chips == 4
     greeted = (1, 2) if relayed else tuple(range(1, chips))
     for s in greeted:
         pl.semaphore_signal(barrier, inc=1, device_id=(partners[s] * 2 + core, mv), device_id_type=MESH)
+    pl.semaphore_signal(barrier, inc=1, device_id=(mate, mv), device_id_type=MESH)
     for s in range(1, nv):
         pl.semaphore_signal(barrier, inc=1, device_id=(me, lax.rem(mv + s, nv)), device_id_type=MESH)
-
+    for load in loads:
+        load.start()
+    loads[0].wait()
     pl.semaphore_wait(barrier, len(greeted) + nv)
 
     def push(owner, part, target, send, recv):
         low, size = part
         here = panel.at[pl.ds(pl.multiple_of(owner * depth + low, 16), size), :]
-        source = int_hbm.at[pl.ds(low, size), :] if owner is me else here
         return pltpu.make_async_remote_copy(
-            src_ref=source, dst_ref=here, send_sem=send, recv_sem=recv,
+            src_ref=here, dst_ref=here, send_sem=send, recv_sem=recv,
             device_id=(target, mv), device_id_type=MESH,
         )
 
@@ -105,18 +106,6 @@
         for s in range(1, chips):
             go(to_chip(s))
     go(to_mate(0))
-    for load in loads:
-        load.start()
-
-    if relayed:
-        from_chip(1, top, 0).wait_recv()
-        go(push(theirs[1], top, theirs[2], chip_send.at[3, 0], chip_recv.at[3, 0]))
-        from_chip(2, bottom, 1).wait_recv()
-        go(push(theirs[2], bottom, theirs[1], chip_send.at[3, 1], chip_recv.at[3, 1]))
-        from_chip(1, bottom, 1).wait_recv()
-        go(to_mate(1))
-        from_chip(2, top, 0).wait_recv()
-        go(to_mate(2))
 
     loads[2].wait()
     loads[3].wait()
@@ -128,8 +117,6 @@
             amp[tall, wide] = amp[tall, wide] * keep
     loads[4].wait()
     loads[5].wait()
-
-    loads[0].wait()
     loads[1].wait()
     span = 2 * depth
     grain = min(span, VTILE)
@@ -151,6 +138,16 @@
         )
 
     if relayed:
+        from_chip(1, top, 0).wait_recv()
+        go(push(theirs[1], top, theirs[2], chip_send.at[3, 0], chip_recv.at[3, 0]))
+        from_chip(2, bottom, 1).wait_recv()
+        go(push(theirs[2], bottom, theirs[1], chip_send.at[3, 1], chip_recv.at[3, 1]))
+        from_chip(1, bottom, 1).wait_recv()
+        go(to_mate(1))
+        from_chip(2, top, 0).wait_recv()
+        go(to_mate(2))
+
+    if relayed:
         from_mate(0).wait_recv()
         acc[...] += product(0)
         push(theirs[3], top, theirs[2], chip_send.at[3, 0], chip_recv.at[3, 0]).wait_recv()
@@ -163,17 +160,13 @@
         from_mate(3, top, 0).wait_recv()
         from_mate(3, bottom, 1).wait_recv()
     else:
-        from_mate(0).wait_recv()
-        if chips > 1:
-            acc[...] += product(0)
         for s in range(1, chips):
             from_chip(s).wait_recv()
             go(to_mate(s))
-            if s > 1:
-                from_mate(s - 1).wait_recv()
-                acc[...] += product(s - 1)
-        if chips > 1:
-            from_mate(chips - 1).wait_recv()
+        for s in range(chips):
+            from_mate(s).wait_recv()
+            if s < chips - 1:
+                acc[...] += product(s)
 
     residual = acc[...] + product(chips - 1)
     out_ref[...] = residual

time: 17.2 us -> 17.3 us (level)
  no operation moved by 1% of the time
where the time goes in v8:
time: 17.3 us; the launch traced here: 17.1 us
  Pallas kernels  16.5 us (95%)
  between operations  0.64 us (4%)
    pallas_call x1, Pallas kernels, on_device(): pl.pallas_call(functools.partial(kernel, n, nv), out_shape=(pltpu.VMEM((r...  15.7 us
    pallas_call x1, Pallas kernels, on_device(): pl.pallas_call(deliver, out_shape=(jax.ShapeDtypeStruct((rows, cols), jnp...  0.81 us

profile of v8, /device:TPU:0, one launch (start us, length us, event | category | flops | bytes accessed | tf_op | source)
XLA Modules:
  0.0 17.1 jit_solution(17422819285907954673)
XLA Ops:
  0.6 15.7 %shard_map.77 = (f32[512,256]{1,0:T(8,128)S(1)}, f32[4,128]{1,0:T(4,128)S(1)}) custom-call(bf16[512,1024]{1,0:T(8,128)(2,1)} %amp_hbm.1, s32[8,8]{1,0:T(8,128)} %amap_hbm.1, bf16[128,256]{1,0:T(8,128)(2,1)} %int_hbm.1, s32[2,8]{1,0:T(2,128)} %bitcast.2, bf16[512,256]{1,0:T(8,128)(2,1)} %exch_hbm.1, f32[512,256]{1,0:T(8,128)} %res_hbm.1), custom_call_target="tpu_custom_call" | custom-call | flops 268435456 | bytes 2883584 | tf_op jit(solution)/shard_map/pallas_call | solution.py:225
  16.3 0.8 %shard_map.78 = (f32[512,256]{1,0:T(8,128)}, f32[4,128]{1,0:T(4,128)}) custom-call(f32[512,256]{1,0:T(8,128)S(1)} %get-tuple-element.6.residual, f32[4,128]{1,0:T(4,128)S(1)} %get-tuple-element.7.energy), custom_call_target="tpu_custom_call" | custom-call | tf_op jit(solution)/shard_map/pallas_call | solution.py:255

commit v9 on v6

--- a/solution.py
+++ b/solution.py
@@ -10,7 +10,7 @@
 PTILE = 64
 VTILE = 128
 LANES = 128
-PARTS = 4
+PARTS = 1
 MESH = pl.DeviceIdType.MESH
 
 
@@ -93,7 +93,7 @@
         copy.start()
         sent.append(copy)
 
-    for s in reversed(range(1, chips)):
+    for s in range(1, chips):
         go(to_chip(s))
     go(to_mate(0))
 
@@ -128,9 +128,12 @@
         )
 
     for s in range(1, chips):
+        if s == chips - 1:
+            from_mate(0).wait_recv()
+            acc[...] += product(0)
         from_chip(s).wait_recv()
         go(to_mate(s))
-    for s in range(chips):
+    for s in range(1, chips):
         from_mate(s).wait_recv()
         if s < chips - 1:
             acc[...] += product(s)

time: 16 us -> 16.3 us (1.019)
  Pallas kernels: 15.2 us -> 15.5 us
    pallas_call x1, Pallas kernels: 14.4 us -> 14.7 us  [on_device(): pl.pallas_call(functools.partial(kernel, n, nv), out_shape=(pltpu.VMEM((r...]
where the time goes in v9:
time: 16.3 us; the launch traced here: 16.1 us
  Pallas kernels  15.5 us (95%)
  between operations  0.64 us (4%)
    pallas_call x1, Pallas kernels, on_device(): pl.pallas_call(functools.partial(kernel, n, nv), out_shape=(pltpu.VMEM((r...  14.7 us
    pallas_call x1, Pallas kernels, on_device(): pl.pallas_call(deliver, out_shape=(jax.ShapeDtypeStruct((rows, cols), jnp...  0.82 us

profile of v9, /device:TPU:0, one launch (start us, length us, event | category | flops | bytes accessed | tf_op | source)
XLA Modules:
  0.0 16.1 jit_solution(5649035645412192119)
XLA Ops:
  0.6 14.7 %shard_map.77 = (f32[512,256]{1,0:T(8,128)S(1)}, f32[4,128]{1,0:T(4,128)S(1)}) custom-call(bf16[512,1024]{1,0:T(8,128)(2,1)} %amp_hbm.1, s32[8,8]{1,0:T(8,128)} %amap_hbm.1, bf16[128,256]{1,0:T(8,128)(2,1)} %int_hbm.1, s32[2,8]{1,0:T(2,128)} %bitcast.2, bf16[512,256]{1,0:T(8,128)(2,1)} %exch_hbm.1, f32[512,256]{1,0:T(8,128)} %res_hbm.1), custom_call_target="tpu_custom_call" | custom-call | flops 268435456 | bytes 2883584 | tf_op jit(solution)/shard_map/pallas_call | solution.py:196
  15.3 0.8 %shard_map.78 = (f32[512,256]{1,0:T(8,128)}, f32[4,128]{1,0:T(4,128)}) custom-call(f32[512,256]{1,0:T(8,128)S(1)} %get-tuple-element.6.residual, f32[4,128]{1,0:T(4,128)S(1)} %get-tuple-element.7.energy), custom_call_target="tpu_custom_call" | custom-call | tf_op jit(solution)/shard_map/pallas_call | solution.py:226

commit v10 on v6

--- a/solution.py
+++ b/solution.py
@@ -10,7 +10,7 @@
 PTILE = 64
 VTILE = 128
 LANES = 128
-PARTS = 4
+PARTS = 1
 MESH = pl.DeviceIdType.MESH
 
 
@@ -97,17 +97,6 @@
         go(to_chip(s))
     go(to_mate(0))
 
-    loads[2].wait()
-    loads[3].wait()
-    for r in range(rows // PTILE):
-        tall = pl.ds(r * PTILE, PTILE)
-        for k in range(amp.shape[1] // VTILE):
-            wide = pl.ds(k * VTILE, VTILE)
-            keep = amap[r, k].astype(jnp.float32).astype(jnp.bfloat16)
-            amp[tall, wide] = amp[tall, wide] * keep
-    loads[4].wait()
-    loads[5].wait()
-    loads[1].wait()
     span = 2 * depth
     grain = min(span, VTILE)
     while span % grain or VTILE % grain:
@@ -130,6 +119,18 @@
     for s in range(1, chips):
         from_chip(s).wait_recv()
         go(to_mate(s))
+
+    loads[2].wait()
+    loads[3].wait()
+    for r in range(rows // PTILE):
+        tall = pl.ds(r * PTILE, PTILE)
+        for k in range(amp.shape[1] // VTILE):
+            wide = pl.ds(k * VTILE, VTILE)
+            keep = amap[r, k].astype(jnp.float32).astype(jnp.bfloat16)
+            amp[tall, wide] = amp[tall, wide] * keep
+    loads[4].wait()
+    loads[5].wait()
+    loads[1].wait()
     for s in range(chips):
         from_mate(s).wait_recv()
         if s < chips - 1:

time: 16 us -> 16.3 us (1.019)
  Pallas kernels: 15.2 us -> 15.5 us
    pallas_call x1, Pallas kernels: 14.4 us -> 14.7 us  [on_device(): pl.pallas_call(functools.partial(kernel, n, nv), out_shape=(pltpu.VMEM((r...]
where the time goes in v10:
time: 16.3 us; the launch traced here: 16.1 us
  Pallas kernels  15.5 us (95%)
  between operations  0.64 us (4%)
    pallas_call x1, Pallas kernels, on_device(): pl.pallas_call(functools.partial(kernel, n, nv), out_shape=(pltpu.VMEM((r...  14.7 us
    pallas_call x1, Pallas kernels, on_device(): pl.pallas_call(deliver, out_shape=(jax.ShapeDtypeStruct((rows, cols), jnp...  0.82 us

profile of v10, /device:TPU:0, one launch (start us, length us, event | category | flops | bytes accessed | tf_op | source)
XLA Modules:
  0.0 16.1 jit_solution(8260208451711771199)
XLA Ops:
  0.6 14.7 %shard_map.77 = (f32[512,256]{1,0:T(8,128)S(1)}, f32[4,128]{1,0:T(4,128)S(1)}) custom-call(bf16[512,1024]{1,0:T(8,128)(2,1)} %amp_hbm.1, s32[8,8]{1,0:T(8,128)} %amap_hbm.1, bf16[128,256]{1,0:T(8,128)(2,1)} %int_hbm.1, s32[2,8]{1,0:T(2,128)} %bitcast.2, bf16[512,256]{1,0:T(8,128)(2,1)} %exch_hbm.1, f32[512,256]{1,0:T(8,128)} %res_hbm.1), custom_call_target="tpu_custom_call" | custom-call | flops 268435456 | bytes 2883584 | tf_op jit(solution)/shard_map/pallas_call | solution.py:194
  15.3 0.8 %shard_map.78 = (f32[512,256]{1,0:T(8,128)}, f32[4,128]{1,0:T(4,128)}) custom-call(f32[512,256]{1,0:T(8,128)S(1)} %get-tuple-element.6.residual, f32[4,128]{1,0:T(4,128)S(1)} %get-tuple-element.7.energy), custom_call_target="tpu_custom_call" | custom-call | tf_op jit(solution)/shard_map/pallas_call | solution.py:224

commit v11 on v6

--- a/solution.py
+++ b/solution.py
@@ -10,7 +10,7 @@
 PTILE = 64
 VTILE = 128
 LANES = 128
-PARTS = 4
+PARTS = 1
 MESH = pl.DeviceIdType.MESH
 
 
@@ -127,10 +127,13 @@
             preferred_element_type=jnp.float32,
         )
 
+    from_mate(0).wait_recv()
+    if chips > 1:
+        acc[...] += product(0)
     for s in range(1, chips):
         from_chip(s).wait_recv()
         go(to_mate(s))
-    for s in range(chips):
+    for s in range(1, chips):
         from_mate(s).wait_recv()
         if s < chips - 1:
             acc[...] += product(s)

time: 16 us -> 15.7 us (0.981)
  Pallas kernels: 15.2 us -> 14.9 us
    pallas_call x1, Pallas kernels: 14.4 us -> 14.1 us  [on_device(): pl.pallas_call(functools.partial(kernel, n, nv), out_shape=(pltpu.VMEM((r...]
where the time goes in v11:
time: 15.7 us; the launch traced here: 15.5 us
  Pallas kernels  14.9 us (95%)
  between operations  0.64 us (4%)
    pallas_call x1, Pallas kernels, on_device(): pl.pallas_call(functools.partial(kernel, n, nv), out_shape=(pltpu.VMEM((r...  14.1 us
    pallas_call x1, Pallas kernels, on_device(): pl.pallas_call(deliver, out_shape=(jax.ShapeDtypeStruct((rows, cols), jnp...  0.82 us

profile of v11, /device:TPU:0, one launch (start us, length us, event | category | flops | bytes accessed | tf_op | source)
XLA Modules:
  0.0 15.5 jit_solution(14849288564284536912)
XLA Ops:
  0.6 14.1 %shard_map.77 = (f32[512,256]{1,0:T(8,128)S(1)}, f32[4,128]{1,0:T(4,128)S(1)}) custom-call(bf16[512,1024]{1,0:T(8,128)(2,1)} %amp_hbm.1, s32[8,8]{1,0:T(8,128)} %amap_hbm.1, bf16[128,256]{1,0:T(8,128)(2,1)} %int_hbm.1, s32[2,8]{1,0:T(2,128)} %bitcast.2, bf16[512,256]{1,0:T(8,128)(2,1)} %exch_hbm.1, f32[512,256]{1,0:T(8,128)} %res_hbm.1), custom_call_target="tpu_custom_call" | custom-call | flops 268435456 | bytes 2883584 | tf_op jit(solution)/shard_map/pallas_call | solution.py:196
  14.7 0.8 %shard_map.78 = (f32[512,256]{1,0:T(8,128)}, f32[4,128]{1,0:T(4,128)}) custom-call(f32[512,256]{1,0:T(8,128)S(1)} %get-tuple-element.6.residual, f32[4,128]{1,0:T(4,128)S(1)} %get-tuple-element.7.energy), custom_call_target="tpu_custom_call" | custom-call | tf_op jit(solution)/shard_map/pallas_call | solution.py:226

commit v12 on v11

--- a/solution.py
+++ b/solution.py
@@ -130,15 +130,15 @@
     from_mate(0).wait_recv()
     if chips > 1:
         acc[...] += product(0)
-    for s in range(1, chips):
+    for s in reversed(range(1, chips)):
         from_chip(s).wait_recv()
         go(to_mate(s))
-    for s in range(1, chips):
+    for s in reversed(range(1, chips)):
         from_mate(s).wait_recv()
-        if s < chips - 1:
+        if s > 1:
             acc[...] += product(s)
 
-    residual = acc[...] + product(chips - 1)
+    residual = acc[...] + product(min(1, chips - 1))
     out_ref[...] = residual
     terms = residual * exch[...].astype(jnp.float32)
     folded = terms[:, :LANES]

time: 15.7 us -> 15.7 us (level)
  no operation moved by 1% of the time
where the time goes in v12:
time: 15.7 us; the launch traced here: 15.5 us
  Pallas kernels  14.9 us (95%)
  between operations  0.64 us (4%)
    pallas_call x1, Pallas kernels, on_device(): pl.pallas_call(functools.partial(kernel, n, nv), out_shape=(pltpu.VMEM((r...  14.1 us
    pallas_call x1, Pallas kernels, on_device(): pl.pallas_call(deliver, out_shape=(jax.ShapeDtypeStruct((rows, cols), jnp...  0.82 us

profile of v12, /device:TPU:0, one launch (start us, length us, event | category | flops | bytes accessed | tf_op | source)
XLA Modules:
  0.0 15.5 jit_solution(5716547606236244107)
XLA Ops:
  0.6 14.1 %shard_map.77 = (f32[512,256]{1,0:T(8,128)S(1)}, f32[4,128]{1,0:T(4,128)S(1)}) custom-call(bf16[512,1024]{1,0:T(8,128)(2,1)} %amp_hbm.1, s32[8,8]{1,0:T(8,128)} %amap_hbm.1, bf16[128,256]{1,0:T(8,128)(2,1)} %int_hbm.1, s32[2,8]{1,0:T(2,128)} %bitcast.2, bf16[512,256]{1,0:T(8,128)(2,1)} %exch_hbm.1, f32[512,256]{1,0:T(8,128)} %res_hbm.1), custom_call_target="tpu_custom_call" | custom-call | flops 268435456 | bytes 2883584 | tf_op jit(solution)/shard_map/pallas_call | solution.py:196
  14.7 0.8 %shard_map.78 = (f32[512,256]{1,0:T(8,128)}, f32[4,128]{1,0:T(4,128)}) custom-call(f32[512,256]{1,0:T(8,128)S(1)} %get-tuple-element.6.residual, f32[4,128]{1,0:T(4,128)S(1)} %get-tuple-element.7.energy), custom_call_target="tpu_custom_call" | custom-call | tf_op jit(solution)/shard_map/pallas_call | solution.py:226
